TPU v7x, 32 devices: a whole 2x2x4 slice. The times are simulated.
32 devices in a mesh: gx: 4 (over x, core), yz: 8 (over z, y).
Axes of the slice: x: 2, y: 2, z: 4, core: 2. Of those that a mesh axis runs over, the one named last changes fastest.
Arguments:
- hidden_in: bfloat16 [2, 32, 8192], P(None, ('gx', 'yz')), may hold values from -6 to 6
- k_cache: bfloat16 [32, 1024, 1024], P(('gx', 'yz'))
- v_cache: bfloat16 [32, 1024, 1024], P(('gx', 'yz')), may hold values from -6 to 6
- lengths: int32 [32], P(('gx', 'yz')), may hold values from 1 to 1024, as said below
- counts: int32 [32, 16], P(('gx', 'yz')), may hold values from 0 to 3
- token_elem: int32 [512], replicated, may hold values from 0 to 16, as said below
- tokens: int32 [32], P(('gx', 'yz')), may hold values from 0 to 511
- attn_gain: float32 [8192], replicated, may hold values from 0.5 to 1.5
- qkv_weight: bfloat16 [8192, 10240], P('gx', 'yz'), may hold values from -0.0625 to 0.0625
- o_weight: bfloat16 [8192, 8192], P('gx', 'yz'), may hold values from -0.0625 to 0.0625
- ffn_gain: float32 [8192], replicated, may hold values from 0.5 to 1.5
- gate_up_weight: bfloat16 [8192, 57344], P('gx', 'yz'), may hold values from -0.0625 to 0.0625
- down_weight: bfloat16 [28672, 8192], P('gx', 'yz'), may hold values from -0.03125 to 0.03125
- final_gain: float32 [8192], replicated, may hold values from 0.5 to 1.5
- lm_weight: bfloat16 [8192, 512], P(('gx', 'yz'))
Outputs:
- layer_out: bfloat16 [2, 32, 8192], P(None, ('gx', 'yz'))
- log_probs: float32 [2, 32, 512], P(None, ('gx', 'yz'))
Inputs may be any that keep to these rules, and one draw needn't show every extreme that they name: `lengths`: some spectrum uses all 1024 positions. `token_elem`: some token has no element (value 16).
All inputs are finite; a program needn't handle non-finite values.
Results may differ from a plain program's by a relative error of at most 0.022.
Values may be sent and summed in bfloat16 or wider, within the bound.
A program may use at most 128 MiB of HBM per device.

v0:
```python
import math

import jax
import jax.numpy as jnp
from jax import lax
from jax.sharding import PartitionSpec as P

FF = 28672
HEADS = 64
KV_HEADS = 8
HEAD = 128
VOCAB = 512
ELEMENTS = 16


NORM_EPS = 1e-05
ROPE_THETA = 500000.0


def norm_rows(values, gain_vec):
    wide = values.astype(jnp.float32)
    inverse = lax.rsqrt(jnp.mean(wide * wide, axis=-1, keepdims=True) + NORM_EPS)
    return (wide * inverse * gain_vec).astype(jnp.bfloat16)


def rotate(heads_in, positions):
    half_width = heads_in.shape[-1] // 2
    frequency = jnp.power(
        ROPE_THETA, -(jnp.arange(half_width, dtype=jnp.float32) * 2.0 / heads_in.shape[-1])
    )
    angles = positions.astype(jnp.float32)[:, None] * frequency[None, :]
    cos_part = jnp.cos(angles)[:, None, :]
    sin_part = jnp.sin(angles)[:, None, :]
    wide = heads_in.astype(jnp.float32)
    first_half = wide[..., :half_width]
    second_half = wide[..., half_width:]
    joined = jnp.concatenate(
        [
            first_half * cos_part - second_half * sin_part,
            second_half * cos_part + first_half * sin_part,
        ],
        -1,
    )
    return joined.astype(jnp.bfloat16)


def spread_rows(inputs):
    gathered = lax.all_gather(inputs, "yz", axis=0, tiled=True)
    return lax.all_to_all(gathered, "gx", split_axis=1, concat_axis=0, tiled=True)


def project(inputs, weight):
    spread = spread_rows(inputs)
    summed = lax.psum_scatter(
        jnp.dot(spread, weight, preferred_element_type=jnp.float32),
        "gx",
        scatter_dimension=0,
        tiled=True,
    )
    return lax.all_to_all(
        summed.astype(jnp.bfloat16), "yz", split_axis=0, concat_axis=1, tiled=True
    )


def head_logits(normed, lm_weight):
    slice_width = lm_weight.shape[0]
    offset_cols = lax.axis_index("yz") * slice_width
    spread = spread_rows(normed)
    own_cols = lax.dynamic_slice_in_dim(spread, offset_cols, slice_width, 1)
    return lax.psum_scatter(
        jnp.dot(own_cols, lm_weight, preferred_element_type=jnp.float32),
        ("gx", "yz"),
        scatter_dimension=0,
        tiled=True,
    )


def attend(queries, k_cache, v_cache, lengths, keys_new, values_new):
    groups = HEADS // KV_HEADS
    factor = 1.0 / math.sqrt(HEAD)
    steps, rows_here = queries.shape[:2]
    cache_len = k_cache.shape[1]
    query_heads = queries.reshape(steps, rows_here, KV_HEADS, groups, HEAD)
    kcache_heads = k_cache.reshape(rows_here, cache_len, KV_HEADS, HEAD)
    vcache_heads = v_cache.reshape(rows_here, cache_len, KV_HEADS, HEAD)
    knew_heads = keys_new.reshape(steps, rows_here, KV_HEADS, HEAD)
    vnew_heads = values_new.reshape(steps, rows_here, KV_HEADS, HEAD)
    scores_cache = (
        jnp.einsum("srkgd,rlkd->srkgl", query_heads, kcache_heads, preferred_element_type=jnp.float32)
        * factor
    )
    valid = jnp.arange(cache_len)[None, None, None, None, :] < lengths[None, :, None, None, None]
    scores_cache = jnp.where(valid, scores_cache, -jnp.inf)
    scores_new = (
        jnp.einsum("srkgd,nrkd->srkgn", query_heads, knew_heads, preferred_element_type=jnp.float32)
        * factor
    )
    order = jnp.arange(steps)
    seen = (order[None, :] <= order[:, None])[:, None, None, None, :]
    scores_new = jnp.where(seen, scores_new, -jnp.inf)
    largest = jnp.maximum(jnp.max(scores_cache, -1), jnp.max(scores_new, -1))[..., None]
    exp_cache = jnp.where(valid, jnp.exp(scores_cache - largest), 0.0)
    exp_new = jnp.where(seen, jnp.exp(scores_new - largest), 0.0)
    denominator = jnp.sum(exp_cache, -1, keepdims=True) + jnp.sum(exp_new, -1, keepdims=True)
    weights_cache = (exp_cache / denominator).astype(jnp.bfloat16)
    weights_new = (exp_new / denominator).astype(jnp.bfloat16)
    result = jnp.einsum(
        "srkgl,rlkd->srkgd", weights_cache, vcache_heads, preferred_element_type=jnp.float32
    )
    result = result + jnp.einsum(
        "srkgn,nrkd->srkgd", weights_new, vnew_heads, preferred_element_type=jnp.float32
    )
    return result.reshape(steps * rows_here, HEADS * HEAD).astype(jnp.bfloat16)


def element_table(token_elem):
    return (token_elem[:, None] == jnp.arange(ELEMENTS, dtype=jnp.int32)[None, :]).astype(
        jnp.float32
    )


def masked_log_probs(logits, remaining, token_elem):
    element_hot = element_table(token_elem)
    per_token = jnp.dot(remaining, element_hot.T)
    allowed = (per_token > 0.5) | (token_elem == ELEMENTS)[None, :]
    largest = jnp.max(jnp.where(allowed, logits, -jnp.inf), -1, keepdims=True)
    shifted = logits - largest
    denominator = jnp.sum(jnp.where(allowed, jnp.exp(shifted), 0.0), -1, keepdims=True)
    return jnp.where(allowed, shifted - jnp.log(denominator), 0.0)


def used_elements(tokens, token_elem):
    token_hot = (tokens[:, None] == jnp.arange(VOCAB, dtype=jnp.int32)[None, :]).astype(jnp.float32)
    return jnp.dot(token_hot, element_table(token_elem))


def per_device(
    hidden_in,
    k_cache,
    v_cache,
    lengths,
    counts,
    token_elem,
    tokens,
    attn_gain,
    qkv_weight,
    o_weight,
    ffn_gain,
    gate_up_weight,
    down_weight,
    final_gain,
    lm_weight,
):
    q_width = HEADS * HEAD
    kv_width = KV_HEADS * HEAD
    steps, rows_here, width = hidden_in.shape
    layer_in = hidden_in.reshape(steps * rows_here, width)
    positions = (jnp.arange(steps, dtype=jnp.int32)[:, None] + lengths[None, :]).reshape(-1)
    mixed = project(norm_rows(layer_in, attn_gain), qkv_weight)
    queries = rotate(mixed[:, :q_width].reshape(-1, HEADS, HEAD), positions)
    keys_now = rotate(
        mixed[:, q_width : q_width + kv_width].reshape(-1, KV_HEADS, HEAD), positions
    )
    values_now = mixed[:, q_width + kv_width :]
    attended = attend(
        queries.reshape(steps, rows_here, q_width),
        k_cache,
        v_cache,
        lengths,
        keys_now.reshape(steps, rows_here, kv_width),
        values_now.reshape(steps, rows_here, kv_width),
    )
    projected = project(attended, o_weight)
    residual = (layer_in.astype(jnp.float32) + projected.astype(jnp.float32)).astype(jnp.bfloat16)
    gate_up = project(norm_rows(residual, ffn_gain), gate_up_weight)
    hidden_units = (
        jax.nn.silu(gate_up[:, :FF].astype(jnp.float32)) * gate_up[:, FF:].astype(jnp.float32)
    ).astype(jnp.bfloat16)
    lowered = project(hidden_units, down_weight)
    result = (residual.astype(jnp.float32) + lowered.astype(jnp.float32)).astype(jnp.bfloat16)
    logits = head_logits(norm_rows(result, final_gain), lm_weight)
    logit_steps = logits.reshape(steps, rows_here, VOCAB)
    outputs = result.reshape(steps, rows_here, width)
    remaining = counts.astype(jnp.float32)
    first_log = masked_log_probs(logit_steps[0], remaining, token_elem)
    remaining = remaining - used_elements(tokens, token_elem)
    second_log = masked_log_probs(logit_steps[1], remaining, token_elem)
    return (outputs, jnp.stack([first_log, second_log]))


def solution(mesh):
    return jax.shard_map(
        per_device,
        mesh=mesh,
        in_specs=(
            P(None, ("gx", "yz"), None),
            P(("gx", "yz"), None, None),
            P(("gx", "yz"), None, None),
            P(("gx", "yz")),
            P(("gx", "yz"), None),
            P(),
            P(("gx", "yz")),
            P(),
            P("gx", "yz"),
            P("gx", "yz"),
            P(),
            P("gx", "yz"),
            P("gx", "yz"),
            P(),
            P(("gx", "yz"), None),
        ),
        out_specs=(P(None, ("gx", "yz"), None), P(None, ("gx", "yz"), None)),
        check_vma=False,
    )
```

profile of v0, /device:TPU:0, one launch (start us, length us, event | category | flops | bytes accessed | tf_op | source)
XLA Modules:
  0.0 527.2 jit_solution(6017064069567963124)
XLA Ops:
  9.1 32.5 %all-gather = bf16[8,2,8192]{2,1,0:T(2,128)(2,1)S(1)} all-gather(bf16[1,2,8192]{2,1,0:T(2,128)(2,1)S(1)} %fusion.60), channel_id=1, replica_groups=mesh['gx'=4,'yz'=8] {'yz'}, dimensions={0}, use_global_device_ids=true | all-gather | bytes 294912 | tf_op jit(solution)/shard_map/all_gather | solution.py:48
  41.9 8.6 %all_to_all.159 = bf16[16,4,2048]{2,0,1:T(8,128)(2,1)S(1)} all-to-all(bf16[16,4,2048]{2,0,1:T(8,128)(2,1)S(1)} %copy.60), channel_id=1, replica_groups=mesh['gx'=4,'yz'=8] {'gx'}, dimensions={1} | all-to-all | bytes 524288 | tf_op jit(solution)/shard_map/all_to_all | solution.py:49
  50.5 4.3 fusion.84
  61.4 14.1 %reduce-scatter.5.cloned.1.call-done = f32[16,1280]{1,0:T(8,128)} async-done(((f32[64,1280]{1,0:T(8,128)}), f32[16,1280]{1,0:T(8,128)}) %reduce-scatter.5.cloned.1.call-update) | async-done | bytes 81936 | tf_op jit(solution)/shard_map/reduce_scatter | solution.py:54
  77.0 5.5 %all-to-all-start.1 = ((bf16[8,2,1280]{2,1,0:T(2,128)(2,1)}), bf16[8,2,1280]{2,1,0:T(2,128)(2,1)S(1)}, u32[]{:S(2)}, u32[]{:S(2)}) async-start(bf16[8,2,1280]{2,1,0:T(2,128)(2,1)} %all_to_all.122), calls=%async_computation.2 | async-start | bytes 81920 | tf_op jit(solution)/shard_map/all_to_all | solution.py:60
  82.6 6.7 %all-to-all-done.1 = bf16[8,2,1280]{2,1,0:T(2,128)(2,1)S(1)} async-done(((bf16[8,2,1280]{2,1,0:T(2,128)(2,1)}), bf16[8,2,1280]{2,1,0:T(2,128)(2,1)S(1)}, u32[]{:S(2)}, u32[]{:S(2)}) %all-to-all-start.1) | async-done | bytes 40992 | tf_op jit(solution)/shard_map/all_to_all | solution.py:60
  92.1 30.8 %all-gather.1 = bf16[8,2,8192]{2,1,0:T(2,128)(2,1)S(1)} all-gather(bf16[1,2,8192]{2,1,0:T(2,128)(2,1)S(1)} %reshape.334), channel_id=1, replica_groups=mesh['gx'=4,'yz'=8] {'yz'}, dimensions={0}, use_global_device_ids=true | all-gather | bytes 294912 | tf_op jit(solution)/shard_map/all_gather | solution.py:48
  123.2 8.4 %all_to_all.160 = bf16[16,4,2048]{2,0,1:T(8,128)(2,1)S(1)} all-to-all(bf16[16,4,2048]{2,0,1:T(8,128)(2,1)S(1)} %copy.66), channel_id=1, replica_groups=mesh['gx'=4,'yz'=8] {'gx'}, dimensions={1} | all-to-all | bytes 524288 | tf_op jit(solution)/shard_map/all_to_all | solution.py:49
  135.4 16.6 %reduce-scatter.7.cloned.1.call-done = f32[16,1024]{1,0:T(8,128)} async-done(((f32[64,1024]{1,0:T(8,128)}), f32[16,1024]{1,0:T(8,128)}) %reduce-scatter.7.cloned.1.call-update) | async-done | bytes 65552 | tf_op jit(solution)/shard_map/reduce_scatter | solution.py:54
  152.9 12.0 %all_to_all.161 = bf16[8,2,1024]{2,1,0:T(2,128)(2,1)S(1)} all-to-all(bf16[8,2,1024]{2,1,0:T(2,128)(2,1)S(1)} %all_to_all.130), channel_id=1, replica_groups=mesh['gx'=4,'yz'=8] {'yz'}, dimensions={0} | all-to-all | bytes 65536 | tf_op jit(solution)/shard_map/all_to_all | solution.py:60
  165.2 30.8 %all-gather.2 = bf16[8,2,8192]{2,1,0:T(2,128)(2,1)S(1)} all-gather(bf16[1,2,8192]{2,1,0:T(2,128)(2,1)S(1)} %fusion.58), channel_id=1, replica_groups=mesh['gx'=4,'yz'=8] {'yz'}, dimensions={0}, use_global_device_ids=true | all-gather | bytes 294912 | tf_op jit(solution)/shard_map/all_gather | solution.py:48
  196.3 8.4 %all_to_all.162 = bf16[16,4,2048]{2,0,1:T(8,128)(2,1)S(1)} all-to-all(bf16[16,4,2048]{2,0,1:T(8,128)(2,1)S(1)} %copy.67), channel_id=1, replica_groups=mesh['gx'=4,'yz'=8] {'gx'}, dimensions={1} | all-to-all | bytes 524288 | tf_op jit(solution)/shard_map/all_to_all | solution.py:49
  204.7 13.3 %fusion.86 = f32[64,7168]{1,0:T(8,128)} fusion(bf16[64,2048]{1,0:T(8,128)(2,1)S(1)} %bitcast.164, bf16[2048,7168]{1,0:T(8,128)(2,1)} %param.26), kind=kOutput, calls=%fused_computation.124 | convolution fusion | flops 1879048192 | bytes 31457280 | tf_op jit(solution)/shard_map/dot_general | solution.py:55
  218.0 26.3 %reduce-scatter.9.cloned.1.call-done = f32[16,7168]{1,0:T(8,128)} async-done(((f32[64,7168]{1,0:T(8,128)}), f32[16,7168]{1,0:T(8,128)}) %reduce-scatter.9.cloned.1.call-update) | async-done | bytes 458768 | tf_op jit(solution)/shard_map/reduce_scatter | solution.py:54
  245.5 13.8 %all_to_all.163 = bf16[8,2,7168]{2,1,0:T(2,128)(2,1)S(1)} all-to-all(bf16[8,2,7168]{2,1,0:T(2,128)(2,1)S(1)} %all_to_all.136), channel_id=1, replica_groups=mesh['gx'=4,'yz'=8] {'yz'}, dimensions={0} | all-to-all | bytes 458752 | tf_op jit(solution)/shard_map/all_to_all | solution.py:60
  259.6 32.6 %all-gather.3 = bf16[8,2,28672]{2,1,0:T(2,128)(2,1)S(1)} all-gather(bf16[1,2,28672]{2,1,0:T(2,128)(2,1)S(1)} %fusion.38), channel_id=1, replica_groups=mesh['gx'=4,'yz'=8] {'yz'}, dimensions={0}, use_global_device_ids=true | all-gather | bytes 1032192 | tf_op jit(solution)/shard_map/all_gather | solution.py:48
  298.4 12.1 %all-to-all-done.6 = bf16[16,4,7168]{2,0,1:T(8,128)(2,1)S(1)} async-done(((bf16[16,4,7168]{2,0,1:T(8,128)(2,1)}), bf16[16,4,7168]{2,0,1:T(8,128)(2,1)S(1)}, u32[]{:S(2)}, u32[]{:S(2)}) %all-to-all-start.6) | async-done | bytes 917536 | tf_op jit(solution)/shard_map/all_to_all | solution.py:49
  310.5 8.6 %fusion.87 = f32[64,1024]{1,0:T(8,128)} fusion(bf16[64,7168]{1,0:T(8,128)(2,1)S(1)} %bitcast.160, bf16[7168,1024]{1,0:T(8,128)(2,1)} %param.27), kind=kOutput, calls=%fused_computation.125 | convolution fusion | flops 939524096 | bytes 15859712 | tf_op jit(solution)/shard_map/dot_general | solution.py:55
  319.8 17.1 %reduce-scatter.11.cloned.1.call-done = f32[16,1024]{1,0:T(8,128)} async-done(((f32[64,1024]{1,0:T(8,128)}), f32[16,1024]{1,0:T(8,128)}) %reduce-scatter.11.cloned.1.call-update) | async-done | bytes 65552 | tf_op jit(solution)/shard_map/reduce_scatter | solution.py:54
  338.4 5.5 %all-to-all-start.7 = ((bf16[8,2,1024]{2,1,0:T(2,128)(2,1)}), bf16[8,2,1024]{2,1,0:T(2,128)(2,1)S(1)}, u32[]{:S(2)}, u32[]{:S(2)}) async-start(bf16[8,2,1024]{2,1,0:T(2,128)(2,1)} %all_to_all.144), calls=%async_computation.11 | async-start | bytes 65536 | tf_op jit(solution)/shard_map/all_to_all | solution.py:60
  343.9 6.7 %all-to-all-done.7 = bf16[8,2,1024]{2,1,0:T(2,128)(2,1)S(1)} async-done(((bf16[8,2,1024]{2,1,0:T(2,128)(2,1)}), bf16[8,2,1024]{2,1,0:T(2,128)(2,1)S(1)}, u32[]{:S(2)}, u32[]{:S(2)}) %all-to-all-start.7) | async-done | bytes 32800 | tf_op jit(solution)/shard_map/all_to_all | solution.py:60
  350.9 30.8 %all-gather.4 = bf16[8,2,8192]{2,1,0:T(2,128)(2,1)S(1)} all-gather(bf16[1,2,8192]{2,1,0:T(2,128)(2,1)S(1)} %fusion.59), channel_id=1, replica_groups=mesh['gx'=4,'yz'=8] {'yz'}, dimensions={0}, use_global_device_ids=true | all-gather | bytes 294912 | tf_op jit(solution)/shard_map/all_gather | solution.py:48
  386.2 5.9 %all-to-all-done.8 = bf16[16,4,2048]{2,0,1:T(8,128)(2,1)S(1)} async-done(((bf16[16,4,2048]{2,0,1:T(8,128)(2,1)}), bf16[16,4,2048]{2,0,1:T(8,128)(2,1)S(1)}, u32[]{:S(2)}, u32[]{:S(2)}) %all-to-all-start.8) | async-done | bytes 262176 | tf_op jit(solution)/shard_map/all_to_all | solution.py:49
  393.7 118.8 %all-reduce.3.cloned.1.call-done = f32[64,512]{1,0:T(8,128)} async-done(((f32[64,512]{1,0:T(8,128)}), f32[64,512]{1,0:T(8,128)}) %all-reduce.3.cloned.1.call-update) | async-done | bytes 131088
  (91 shorter events, 40.1 us)
Async XLA Ops:
  7.2 385.0 %copy-start = (bf16[256,512]{1,0:T(8,128)(2,1)S(1)}, bf16[256,512]{1,0:T(8,128)(2,1)}, u32[]{:S(2)}) copy-start(bf16[256,512]{1,0:T(8,128)(2,1)} %param.29) | copy-start | bytes 786436
  7.2 68.3 %reduce-scatter.5.cloned.1.call-start = ((), (), s32[]{:S(2)}) async-start(), calls=%async_computation.13 | async-start | bytes 409600 | tf_op jit(solution)/shard_map/reduce_scatter | solution.py:54
  77.0 12.2 %all-to-all-start.1 = ((bf16[8,2,1280]{2,1,0:T(2,128)(2,1)}), bf16[8,2,1280]{2,1,0:T(2,128)(2,1)S(1)}, u32[]{:S(2)}, u32[]{:S(2)}) async-start(bf16[8,2,1280]{2,1,0:T(2,128)(2,1)} %all_to_all.122), calls=%async_computation.2 | async-start | bytes 81920 | tf_op jit(solution)/shard_map/all_to_all | solution.py:60
  82.5 69.5 %reduce-scatter.7.cloned.1.call-start = ((), (), s32[]{:S(2)}) async-start(), calls=%async_computation.14 | async-start | bytes 327680 | tf_op jit(solution)/shard_map/reduce_scatter | solution.py:54
  89.3 1.8 copy-start.1
  91.7 73.1 %copy-start.2 = (bf16[2,1,8192]{2,0,1:T(2,128)(2,1)S(1)}, bf16[2,1,8192]{2,0,1:T(2,128)(2,1)}, u32[]{:S(2)}) copy-start(bf16[2,1,8192]{2,0,1:T(2,128)(2,1)} %param.15) | copy-start | bytes 98308
  91.7 73.3 %copy-start.3 = (f32[8192]{0:T(1024)S(1)}, f32[8192]{0:T(1024)}, u32[]{:S(2)}) copy-start(f32[8192]{0:T(1024)} %param.25) | copy-start | bytes 98308
  135.3 109.0 %reduce-scatter.9.cloned.1.call-start = ((), (), s32[]{:S(2)}) async-start(), calls=%async_computation.15 | async-start | bytes 2293760 | tf_op jit(solution)/shard_map/reduce_scatter | solution.py:54
  294.0 16.5 %all-to-all-start.6 = ((bf16[16,4,7168]{2,0,1:T(8,128)(2,1)}), bf16[16,4,7168]{2,0,1:T(8,128)(2,1)S(1)}, u32[]{:S(2)}, u32[]{:S(2)}) async-start(bf16[16,4,7168]{2,0,1:T(8,128)(2,1)} %copy.68), calls=%async_computation.9 | async-start | bytes 1835008 | tf_op jit(solution)/shard_map/all_to_all | solution.py:49
  297.5 39.4 %reduce-scatter.11.cloned.1.call-start = ((), (), s32[]{:S(2)}) async-start(), calls=%async_computation.16 | async-start | bytes 327680 | tf_op jit(solution)/shard_map/reduce_scatter | solution.py:54
  310.5 8.6 %copy-start.5 = (s32[512]{0:T(512)S(1)}, s32[512]{0:T(512)}, u32[]{:S(2)}) copy-start(s32[512]{0:T(512)} %param.20) | copy-start | bytes 6148
  310.5 8.6 %copy-start.6 = (s32[1,16]{1,0:T(1,128)S(1)}, s32[1,16]{1,0:T(1,128)}, u32[]{:S(2)}) copy-start(s32[1,16]{1,0:T(1,128)} %param.19) | copy-start | bytes 196
  310.5 40.3 %copy-start.4 = (f32[8192]{0:T(1024)S(1)}, f32[8192]{0:T(1024)}, u32[]{:S(2)}) copy-start(f32[8192]{0:T(1024)} %param.28) | copy-start | bytes 98308
  338.4 12.2 %all-to-all-start.7 = ((bf16[8,2,1024]{2,1,0:T(2,128)(2,1)}), bf16[8,2,1024]{2,1,0:T(2,128)(2,1)S(1)}, u32[]{:S(2)}, u32[]{:S(2)}) async-start(bf16[8,2,1024]{2,1,0:T(2,128)(2,1)} %all_to_all.144), calls=%async_computation.11 | async-start | bytes 65536 | tf_op jit(solution)/shard_map/all_to_all | solution.py:60
  382.8 9.4 %all-to-all-start.8 = ((bf16[16,4,2048]{2,0,1:T(8,128)(2,1)}), bf16[16,4,2048]{2,0,1:T(8,128)(2,1)S(1)}, u32[]{:S(2)}, u32[]{:S(2)}) async-start(bf16[16,4,2048]{2,0,1:T(8,128)(2,1)} %copy.69), calls=%async_computation.12 | async-start | bytes 524288 | tf_op jit(solution)/shard_map/all_to_all | solution.py:49
  386.2 126.4 %all-reduce.3.cloned.1.call-start = ((), (), s32[]{:S(2)}) async-start(), calls=%async_computation.17 | async-start | bytes 262144
Sparse Core Ops, SparseCore 0:
  54.9 20.5 reduce-scatter.4
  135.5 16.4 reduce-scatter.6
  218.1 26.1 reduce-scatter.8
  319.2 17.6 reduce-scatter.10
  393.1 119.3 all-reduce.2
where the time goes:
time: 528 us; the launch traced here: 527 us
  waiting for transfers between devices  225 us (43%)
  blocking collectives  209 us (40%)
  matrix products  33.3 us (6%)
  starting transfers between devices  18.3 us (3%)
  between operations  16.8 us (3%)
  other arithmetic  14.5 us (3%)
  local copies, waits for them, and re-layouts  11 us (2%)
    all_gather x5, blocking collectives, spread_rows(): gathered = lax.all_gather(inputs, 'yz', axis=0, tiled=True)  158 us
    unnamed x6, waiting for transfers between devices  119 us
    reduce_scatter x4, waiting for transfers between devices, project(): lax.psum_scatter(jnp.dot(spread, weight, preferred_element_type=jnp.float...  74.2 us
    dot_general x4, matrix products, project(): jnp.dot(spread, weight, preferred_element_type=jnp.float32)  29.8 us
    all_to_all x2, blocking collectives, project(): lax.all_to_all(summed.astype(jnp.bfloat16), 'yz', split_axis=0, concat_ax...  25.7 us
    all_to_all x3, blocking collectives, spread_rows(): lax.all_to_all(gathered, 'gx', split_axis=1, concat_axis=0, tiled=True)  25.4 us
    all_to_all x2, waiting for transfers between devices, spread_rows(): lax.all_to_all(gathered, 'gx', split_axis=1, concat_axis=0, tiled=True)  18.1 us
    all_to_all x2, waiting for transfers between devices, project(): lax.all_to_all(summed.astype(jnp.bfloat16), 'yz', split_axis=0, concat_ax...  13.4 us
  transfers between devices with their start and end apart: 9, of which 9 were waited for; matrix products, arithmetic and copies ran while one was open for 1% of the time, Pallas kernels for 0%

commit v1 on v0

--- a/solution.py
+++ b/solution.py
@@ -1,8 +1,11 @@
+import functools
 import math
 
 import jax
 import jax.numpy as jnp
 from jax import lax
+from jax.experimental import pallas as pl
+from jax.experimental.pallas import tpu as pltpu
 from jax.sharding import PartitionSpec as P
 
 FF = 28672
@@ -44,35 +47,283 @@
     return joined.astype(jnp.bfloat16)
 
 
-def spread_rows(inputs):
-    gathered = lax.all_gather(inputs, "yz", axis=0, tiled=True)
-    return lax.all_to_all(gathered, "gx", split_axis=1, concat_axis=0, tiled=True)
-
-
-def project(inputs, weight):
-    spread = spread_rows(inputs)
-    summed = lax.psum_scatter(
-        jnp.dot(spread, weight, preferred_element_type=jnp.float32),
-        "gx",
-        scatter_dimension=0,
-        tiled=True,
-    )
-    return lax.all_to_all(
-        summed.astype(jnp.bfloat16), "yz", split_axis=0, concat_axis=1, tiled=True
-    )
-
-
-def head_logits(normed, lm_weight):
-    slice_width = lm_weight.shape[0]
-    offset_cols = lax.axis_index("yz") * slice_width
-    spread = spread_rows(normed)
-    own_cols = lax.dynamic_slice_in_dim(spread, offset_cols, slice_width, 1)
-    return lax.psum_scatter(
-        jnp.dot(own_cols, lm_weight, preferred_element_type=jnp.float32),
-        ("gx", "yz"),
-        scatter_dimension=0,
-        tiled=True,
-    )
+def project_kernel(
+    nx,
+    ny,
+    head,
+    tile,
+    x_ref,
+    w_ref,
+    out_ref,
+    wbuf,
+    x1,
+    strips,
+    slot,
+    xall,
+    xmat,
+    pbuf,
+    rbuf,
+    sbuf,
+    obuf,
+    wsem,
+    ssem1,
+    rsem1,
+    ssem2,
+    rsem2,
+    ssem3,
+    rsem3,
+    ssem4,
+    rsem4,
+):
+    gx = lax.axis_index("gx")
+    yz = lax.axis_index("yz")
+    count = wbuf.shape[0]
+    rows = x1.shape[1]
+    mesh_id = pl.DeviceIdType.MESH
+
+    def fetch(c):
+        cols = pl.ds(pl.multiple_of(c * tile, tile), tile)
+        return pltpu.make_async_copy(w_ref.at[:, cols], wbuf.at[c], wsem.at[c])
+
+    def begin(c, carry):
+        fetch(c).start()
+        return carry
+
+    lax.fori_loop(0, count, begin, 0)
+
+    home = yz // 2
+    barrier = pltpu.get_barrier_semaphore()
+    for d in range(1, nx):
+        pl.semaphore_signal(
+            barrier, inc=1, device_id=(lax.rem(gx + d, nx), yz), device_id_type=mesh_id
+        )
+    for d in range(1, ny):
+        pl.semaphore_signal(
+            barrier, inc=1, device_id=(gx, lax.rem(yz + d, ny)), device_id_type=mesh_id
+        )
+    for jj in range(ny):
+        @pl.when(jnp.logical_not((home == gx) & (yz == jj)))
+        def _():
+            pl.semaphore_signal(barrier, inc=1, device_id=(home, jj), device_id_type=mesh_id)
+    apart = (lax.rem(home + nx - gx, nx) + nx - 2) // (nx - 1)
+    pl.semaphore_wait(barrier, nx - 1 + ny - 1 + ny - 1 + apart)
+
+    def first(d):
+        to = lax.rem(gx + d, nx)
+        return pltpu.make_async_remote_copy(
+            src_ref=x_ref.at[to],
+            dst_ref=x1.at[gx],
+            send_sem=ssem1.at[d],
+            recv_sem=rsem1.at[d],
+            device_id=(to, yz),
+            device_id_type=mesh_id,
+        )
+
+    def first_in(d):
+        return pltpu.make_async_remote_copy(
+            src_ref=x_ref.at[gx],
+            dst_ref=x1.at[lax.rem(gx + nx - d, nx)],
+            send_sem=ssem1.at[d],
+            recv_sem=rsem1.at[d],
+            device_id=(lax.rem(gx + d, nx), yz),
+            device_id_type=mesh_id,
+        )
+
+    for d in range(1, nx):
+        first(d).start()
+    x1[gx] = x_ref[gx]
+    for d in range(1, nx):
+        first_in(d).wait_recv()
+    for g in range(nx):
+        strips[g * rows : (g + 1) * rows, :] = x1[g].astype(jnp.float32)
+    if head:
+        width = xmat.shape[1]
+        for jj in range(ny):
+            slot[jj] = strips[:, jj * width : (jj + 1) * width].astype(jnp.bfloat16)
+        xall[yz] = slot[yz]
+    else:
+        slot[0] = strips[...].astype(jnp.bfloat16)
+        xall[yz] = slot[0]
+
+    def second(d):
+        to = lax.rem(yz + d, ny)
+        return pltpu.make_async_remote_copy(
+            src_ref=slot.at[to] if head else slot.at[0],
+            dst_ref=xall.at[yz],
+            send_sem=ssem2.at[d],
+            recv_sem=rsem2.at[d],
+            device_id=(gx, to),
+            device_id_type=mesh_id,
+        )
+
+    def second_in(d):
+        return pltpu.make_async_remote_copy(
+            src_ref=slot.at[0],
+            dst_ref=xall.at[lax.rem(yz + ny - d, ny)],
+            send_sem=ssem2.at[d],
+            recv_sem=rsem2.at[d],
+            device_id=(gx, lax.rem(yz + d, ny)),
+            device_id_type=mesh_id,
+        )
+
+    for d in range(1, ny):
+        second(d).start()
+    for d in range(1, ny):
+        second_in(d).wait_recv()
+    group = 2 * nx * rows
+    for t in range(ny // 2):
+        xmat[t * group : (t + 1) * group, :] = jnp.concatenate(
+            [xall[2 * t].astype(jnp.float32), xall[2 * t + 1].astype(jnp.float32)], 0
+        ).astype(jnp.bfloat16)
+
+    def third(c, d):
+        cols = pl.ds(pl.multiple_of(c * tile, tile), tile)
+        to = lax.rem(gx + d, nx)
+        return pltpu.make_async_remote_copy(
+            src_ref=pbuf.at[to, :, cols],
+            dst_ref=rbuf.at[d, :, cols],
+            send_sem=ssem3.at[c, d],
+            recv_sem=rsem3.at[c, d],
+            device_id=(to, yz),
+            device_id_type=mesh_id,
+        )
+
+    def multiply(c, carry):
+        cols = pl.ds(pl.multiple_of(c * tile, tile), tile)
+        fetch(c).wait()
+        product = jnp.dot(xmat[...], wbuf[c], preferred_element_type=jnp.float32)
+        for t in range(nx):
+            pbuf[t, :, cols] = product[t * group : (t + 1) * group].astype(pbuf.dtype)
+        for d in range(1, nx):
+            third(c, d).start()
+        return carry
+
+    lax.fori_loop(0, count, multiply, 0)
+
+    def reduce(c, carry):
+        cols = pl.ds(pl.multiple_of(c * tile, tile), tile)
+        for d in range(1, nx):
+            third(c, d).wait_recv()
+        total = pbuf[gx, :, cols].astype(jnp.float32)
+        for d in range(1, nx):
+            total = total + rbuf[d, :, cols].astype(jnp.float32)
+        for k in range(2 * nx):
+            sbuf[k, :, cols] = total[k * rows : (k + 1) * rows].astype(sbuf.dtype)
+        return carry
+
+    lax.fori_loop(0, count, reduce, 0)
+
+    def fourth(k, u, g):
+        return pltpu.make_async_remote_copy(
+            src_ref=sbuf.at[k],
+            dst_ref=obuf.at[yz],
+            send_sem=ssem4.at[k],
+            recv_sem=rsem4.at[yz],
+            device_id=(g, 2 * gx + u),
+            device_id_type=mesh_id,
+        )
+
+    def fourth_in(jj):
+        return pltpu.make_async_remote_copy(
+            src_ref=sbuf.at[0],
+            dst_ref=obuf.at[jj],
+            send_sem=ssem4.at[0],
+            recv_sem=rsem4.at[jj],
+            device_id=(lax.rem(gx + 1, nx), yz),
+            device_id_type=mesh_id,
+        )
+
+    for u in range(2):
+        for g in range(nx):
+            mine = (gx == g) & (yz == 2 * gx + u)
+
+            @pl.when(jnp.logical_not(mine))
+            def _():
+                fourth(u * nx + g, u, g).start()
+
+            @pl.when(mine)
+            def _():
+                obuf[yz] = sbuf[u * nx + g]
+
+    for jj in range(ny):
+        @pl.when(jnp.logical_not((home == gx) & (yz == jj)))
+        def _():
+            fourth_in(jj).wait_recv()
+    if head:
+        out_ref[...] = sum(obuf[jj] for jj in range(ny))
+    else:
+        size = obuf.shape[2]
+        for jj in range(ny):
+            out_ref[:, jj * size : (jj + 1) * size] = obuf[jj]
+
+    for d in range(1, nx):
+        first(d).wait_send()
+    for d in range(1, ny):
+        second(d).wait_send()
+
+    def drain(c, carry):
+        for d in range(1, nx):
+            third(c, d).wait_send()
+        return carry
+
+    lax.fori_loop(0, count, drain, 0)
+    for u in range(2):
+        for g in range(nx):
+            @pl.when(jnp.logical_not((gx == g) & (yz == 2 * gx + u)))
+            def _():
+                fourth(u * nx + g, u, g).wait_send()
+
+
+def project(inputs, weight, nx, ny, call_id, head=False):
+    rows, features = inputs.shape
+    depth = features // nx
+    part = depth // ny if head else depth
+    width = weight.shape[1]
+    wire = jnp.float32 if head else jnp.bfloat16
+    limit = 256 if part > 2048 else 512
+    tile = max(t for t in (128, 256, 512) if t <= limit and width % t == 0)
+    count = width // tile
+    group = 2 * nx * rows
+    dma = pltpu.SemaphoreType.DMA
+    blocks = inputs.reshape(rows, nx, depth).transpose(1, 0, 2)
+    return pl.pallas_call(
+        functools.partial(project_kernel, nx, ny, head, tile),
+        out_shape=jax.ShapeDtypeStruct((rows, width if head else ny * width), wire),
+        in_specs=[
+            pl.BlockSpec(memory_space=pltpu.VMEM),
+            pl.BlockSpec(memory_space=pl.ANY),
+        ],
+        out_specs=pl.BlockSpec(memory_space=pltpu.VMEM),
+        scratch_shapes=[
+            pltpu.VMEM((count, part, tile), jnp.bfloat16),
+            pltpu.VMEM((nx, rows, depth), jnp.bfloat16),
+            pltpu.VMEM((nx * rows, depth), jnp.float32),
+            pltpu.VMEM((ny if head else 1, nx * rows, part), jnp.bfloat16),
+            pltpu.VMEM((ny, nx * rows, part), jnp.bfloat16),
+            pltpu.VMEM((ny * nx * rows, part), jnp.bfloat16),
+            pltpu.VMEM((nx, group, width), wire),
+            pltpu.VMEM((nx, group, width), wire),
+            pltpu.VMEM((2 * nx, rows, width), wire),
+            pltpu.VMEM((ny, rows, width), wire),
+            dma((count,)),
+            dma((nx,)),
+            dma((nx,)),
+            dma((ny,)),
+            dma((ny,)),
+            dma((count, nx)),
+            dma((count, nx)),
+            dma((2 * nx,)),
+            dma((ny,)),
+        ],
+        compiler_params=pltpu.CompilerParams(
+            collective_id=call_id, has_side_effects=True, vmem_limit_bytes=56 * 1024 * 1024
+        ),
+        cost_estimate=pl.CostEstimate(
+            flops=2 * ny * nx * rows * part * width,
+            bytes_accessed=2 * part * width,
+            transcendentals=0,
+        ),
+    )(blocks, weight)
 
 
 def attend(queries, k_cache, v_cache, lengths, keys_new, values_new):
@@ -135,6 +386,8 @@
 
 
 def per_device(
+    nx,
+    ny,
     hidden_in,
     k_cache,
     v_cache,
@@ -156,7 +409,7 @@
     steps, rows_here, width = hidden_in.shape
     layer_in = hidden_in.reshape(steps * rows_here, width)
     positions = (jnp.arange(steps, dtype=jnp.int32)[:, None] + lengths[None, :]).reshape(-1)
-    mixed = project(norm_rows(layer_in, attn_gain), qkv_weight)
+    mixed = project(norm_rows(layer_in, attn_gain), qkv_weight, nx, ny, 0)
     queries = rotate(mixed[:, :q_width].reshape(-1, HEADS, HEAD), positions)
     keys_now = rotate(
         mixed[:, q_width : q_width + kv_width].reshape(-1, KV_HEADS, HEAD), positions
@@ -170,15 +423,15 @@
         keys_now.reshape(steps, rows_here, kv_width),
         values_now.reshape(steps, rows_here, kv_width),
     )
-    projected = project(attended, o_weight)
+    projected = project(attended, o_weight, nx, ny, 1)
     residual = (layer_in.astype(jnp.float32) + projected.astype(jnp.float32)).astype(jnp.bfloat16)
-    gate_up = project(norm_rows(residual, ffn_gain), gate_up_weight)
+    gate_up = project(norm_rows(residual, ffn_gain), gate_up_weight, nx, ny, 2)
     hidden_units = (
         jax.nn.silu(gate_up[:, :FF].astype(jnp.float32)) * gate_up[:, FF:].astype(jnp.float32)
     ).astype(jnp.bfloat16)
-    lowered = project(hidden_units, down_weight)
+    lowered = project(hidden_units, down_weight, nx, ny, 3)
     result = (residual.astype(jnp.float32) + lowered.astype(jnp.float32)).astype(jnp.bfloat16)
-    logits = head_logits(norm_rows(result, final_gain), lm_weight)
+    logits = project(norm_rows(result, final_gain), lm_weight, nx, ny, 4, head=True)
     logit_steps = logits.reshape(steps, rows_here, VOCAB)
     outputs = result.reshape(steps, rows_here, width)
     remaining = counts.astype(jnp.float32)
@@ -190,7 +443,7 @@
 
 def solution(mesh):
     return jax.shard_map(
-        per_device,
+        functools.partial(per_device, mesh.shape["gx"], mesh.shape["yz"]),
         mesh=mesh,
         in_specs=(
             P(None, ("gx", "yz"), None),

time: 528 us -> 176 us (0.33)
  waiting for transfers between devices: 225 us -> 0 us
  blocking collectives: 209 us -> 0 us
  Pallas kernels: 0 us -> 148 us
  matrix products: 33.3 us -> 3.4 us
  starting transfers between devices: 18.3 us -> 0 us
  between operations: 16.8 us -> 3.46 us
  local copies, waits for them, and re-layouts: 11 us -> 3.16 us
    all_gather x5 -> x0, blocking collectives: 158 us -> none  [spread_rows(): gathered = lax.all_gather(inputs, 'yz', axis=0, tiled=True)]
    pallas_call x0 -> x5, Pallas kernels: none -> 148 us  [project(): pl.pallas_call(functools.partial(project_kernel, nx, ny, head, tile), out...]
    unnamed x6 -> x0, waiting for transfers between devices: 119 us -> none
    reduce_scatter x4 -> x0, waiting for transfers between devices: 74.2 us -> none  [project(): lax.psum_scatter(jnp.dot(spread, weight, preferred_element_type=jnp.float...]
    all_to_all x5 -> x0, blocking collectives: 51.2 us -> none  [the longest x2 25.7 us: project(): lax.all_to_all(summed.astype(jnp.bfloat16), 'yz', split_axis=0, concat_ax...]
    all_to_all x4 -> x0, waiting for transfers between devices: 31.4 us -> none  [the longest x2 18.1 us: spread_rows(): lax.all_to_all(gathered, 'gx', split_axis=1, concat_axis=0, tiled=True)]
    dot_general x5 -> x0, matrix products: 30.6 us -> none  [the longest x4 29.8 us: project(): jnp.dot(spread, weight, preferred_element_type=jnp.float32)]
    all_to_all x4 -> x0, starting transfers between devices: 17.9 us -> none  [the longest x2 11 us: project(): lax.all_to_all(summed.astype(jnp.bfloat16), 'yz', split_axis=0, concat_ax...]
  transfers between devices with their start and end apart: 9 -> 0, of which waited for: 9 -> 0; matrix products, arithmetic and copies ran while one was open for 1% -> 0% of each run, Pallas kernels for 0% -> 0%
where the time goes in v1:
time: 176 us; the launch traced here: 175 us
  Pallas kernels  148 us (84%)
  other arithmetic  17.4 us (10%)
  between operations  3.46 us (2%)
  matrix products  3.4 us (2%)
  local copies, waits for them, and re-layouts  3.16 us (2%)
    pallas_call x5, Pallas kernels, project(): pl.pallas_call(functools.partial(project_kernel, nx, ny, head, tile), out...  148 us

profile of v1, /device:TPU:0, one launch (start us, length us, event | category | flops | bytes accessed | tf_op | source)
XLA Modules:
  0.0 175.3 jit_solution(14739863820640732193)
XLA Ops:
  1.4 0.8 mul.182
  2.2 0.9 fusion.45
  3.1 1.5 fusion.49.x_ref
  4.6 27.3 %shard_map.158 = bf16[2,10240]{1,0:T(2,128)(2,1)} custom-call(bf16[4,2,2048]{2,1,0:T(2,128)(2,1)} %fusion.49.x_ref, bf16[2048,1280]{1,0:T(8,128)(2,1)} %w_ref.5), custom_call_target="tpu_custom_call" | custom-call | flops 335544320 | bytes 5242880 | tf_op jit(solution)/shard_map/pallas_call | solution.py:289
  31.9 0.8 convert_bitcast_fusion
  32.8 0.7 bitcast_convert_fusion
  33.9 0.6 copy.45
  34.6 0.8 fusion.71
  36.1 0.6 copy.46
  36.8 0.7 fusion.16
  37.5 1.0 fusion.20
  38.5 0.6 copy.74
  39.1 23.0 %shard_map.159 = bf16[2,8192]{1,0:T(2,128)(2,1)} custom-call(bf16[4,2,2048]{2,1,0:T(2,128)(2,1)} %bitcast.129, bf16[2048,1024]{1,0:T(8,128)(2,1)} %w_ref.6), custom_call_target="tpu_custom_call" | custom-call | flops 268435456 | bytes 4194304 | tf_op jit(solution)/shard_map/pallas_call | solution.py:289
  62.2 0.9 fusion.41
  63.1 1.5 fusion.43
  64.6 33.1 %shard_map.160 = bf16[2,57344]{1,0:T(2,128)(2,1)} custom-call(bf16[4,2,2048]{2,1,0:T(2,128)(2,1)} %bitcast.130, bf16[2048,7168]{1,0:T(8,128)(2,1)} %w_ref.7), custom_call_target="tpu_custom_call" | custom-call | flops 1879048192 | bytes 29360128 | tf_op jit(solution)/shard_map/pallas_call | solution.py:289
  97.7 1.9 %fusion.34 = bf16[2,28672]{1,0:T(2,128)(2,1)} fusion(bf16[2,57344]{1,0:T(2,128)(2,1)} %shard_map.160), kind=kLoop, calls=%fused_computation.32 | loop fusion | flops 458752 | bytes 344064 | tf_op jit(solution)/shard_map/convert_element_type | solution.py:431
  99.6 46.6 %shard_map.161 = bf16[2,8192]{1,0:T(2,128)(2,1)} custom-call(bf16[4,2,7168]{2,1,0:T(2,128)(2,1)} %bitcast.128, bf16[7168,1024]{1,0:T(8,128)(2,1)} %w_ref.8), custom_call_target="tpu_custom_call" | custom-call | flops 939524096 | bytes 14680064 | tf_op jit(solution)/shard_map/pallas_call | solution.py:289
  146.2 1.0 fusion.38
  147.2 0.7 fusion.40
  147.9 17.9 %shard_map.162 = f32[2,512]{1,0:T(2,128)} custom-call(bf16[4,2,2048]{2,1,0:T(2,128)(2,1)} %bitcast.131, bf16[256,512]{1,0:T(8,128)(2,1)} %w_ref.9), custom_call_target="tpu_custom_call" | custom-call | flops 16777216 | bytes 262144 | tf_op jit(solution)/shard_map/pallas_call | solution.py:289
  167.1 1.4 fusion.57
  168.6 2.8 %fusion.58 = (f32[]{:T(128)}, f32[]{:T(128)}) fusion(pred[512]{0:T(512)(128)(4,1)S(1)} %get-tuple-element.8, f32[]{:T(128)} %get-tuple-element.4, f32[2,512]{1,0:T(2,128)} %shard_map.162, f32[]{:T(128)} %get-tuple-element.5, pred[512]{0:T(512)(128)(4,1)S(1)} %compare_or_fusion), kind=kLoop, calls=%fused_computation.83 | loop fusion | flops 3070 | bytes 5136 | tf_op jit(solution)/shard_map/reduce_sum | solution.py:379
  172.6 2.1 %fusion.59 = (f32[1,1,512]{2,1,0:T(1,128)S(1)}, f32[1,1,512]{2,1,0:T(1,128)S(1)}) fusion(pred[512]{0:T(512)(128)(4,1)S(1)} %get-tuple-element.8, f32[]{:T(128)S(6)} %log.8, f32[]{:T(128)} %get-tuple-element.4, f32[2,512]{1,0:T(2,128)} %shard_map.162, f32[]{:T(128)S(6)} %log.9, f32[]{:T(128)} %get-tuple-element.5, pred[512]{0:T(512)(128)(4,1)S(1)} %compare_or_fusion), kind=kLoop, calls=%fused_computation.84 | loop fusion | flops 3072 | bytes 9232 | tf_op jit(solution)/shard_map/stack | solution.py:441
  (43 shorter events, 2.8 us)
Async XLA Ops:
  4.6 29.3 %copy-start = (bf16[1,1024,1024]{2,1,0:T(8,128)(2,1)S(1)}, bf16[1,1024,1024]{2,1,0:T(8,128)(2,1)}, u32[]{:S(2)}) copy-start(bf16[1,1024,1024]{2,1,0:T(8,128)(2,1)} %param.16) | copy-start | bytes 6291460
  34.5 1.6 copy-start.1
  39.1 23.0 %copy-start.2 = (bf16[2,1,8192]{2,0,1:T(2,128)(2,1)S(1)}, bf16[2,1,8192]{2,0,1:T(2,128)(2,1)}, u32[]{:S(2)}) copy-start(bf16[2,1,8192]{2,0,1:T(2,128)(2,1)} %param.15) | copy-start | bytes 98308
  39.1 24.0 %copy-start.6 = (f32[8192]{0:T(1024)S(1)}, f32[8192]{0:T(1024)}, u32[]{:S(2)}) copy-start(f32[8192]{0:T(1024)} %param.25) | copy-start | bytes 98308
  99.5 46.6 %copy-start.3 = (bf16[2,8192]{1,0:T(2,128)(2,1)S(1)}, bf16[2,8192]{1,0:T(2,128)(2,1)}, u32[]{:S(2)}) copy-start(bf16[2,8192]{1,0:T(2,128)(2,1)} %shard_map.159) | copy-start | bytes 98308
  99.5 47.6 %copy-start.5 = (f32[8192]{0:T(1024)S(1)}, f32[8192]{0:T(1024)}, u32[]{:S(2)}) copy-start(f32[8192]{0:T(1024)} %param.28) | copy-start | bytes 98308
  99.5 66.3 %copy-start.7 = (s32[512]{0:T(512)S(1)}, s32[512]{0:T(512)}, u32[]{:S(2)}) copy-start(s32[512]{0:T(512)} %param.20) | copy-start | bytes 6148
  99.5 66.3 %copy-start.8 = (s32[1,16]{1,0:T(1,128)S(1)}, s32[1,16]{1,0:T(1,128)}, u32[]{:S(2)}) copy-start(s32[1,16]{1,0:T(1,128)} %param.19) | copy-start | bytes 196
  147.1 28.2 %copy-start.4 = (bf16[2,8192]{1,0:T(2,128)(2,1)}, bf16[2,8192]{1,0:T(2,128)(2,1)S(1)}, u32[]{:S(2)}) copy-start(bf16[2,8192]{1,0:T(2,128)(2,1)S(1)} %get-tuple-element.7) | copy-start | bytes 98308

commit v2 on v1

--- a/solution.py
+++ b/solution.py
@@ -432,13 +432,12 @@
     lowered = project(hidden_units, down_weight, nx, ny, 3)
     result = (residual.astype(jnp.float32) + lowered.astype(jnp.float32)).astype(jnp.bfloat16)
     logits = project(norm_rows(result, final_gain), lm_weight, nx, ny, 4, head=True)
-    logit_steps = logits.reshape(steps, rows_here, VOCAB)
     outputs = result.reshape(steps, rows_here, width)
-    remaining = counts.astype(jnp.float32)
-    first_log = masked_log_probs(logit_steps[0], remaining, token_elem)
-    remaining = remaining - used_elements(tokens, token_elem)
-    second_log = masked_log_probs(logit_steps[1], remaining, token_elem)
-    return (outputs, jnp.stack([first_log, second_log]))
+    first_left = counts.astype(jnp.float32)
+    second_left = first_left - used_elements(tokens, token_elem)
+    remaining = jnp.concatenate([first_left, second_left], 0)
+    logs = masked_log_probs(logits, remaining, token_elem)
+    return (outputs, logs.reshape(steps, rows_here, VOCAB))
 
 
 def solution(mesh):

time: 176 us -> 171 us (0.972)
  other arithmetic: 17.4 us -> 12.1 us
    another operation x3 -> x1, other arithmetic: 2.77 us -> 0.08 us  [the longest x2 2.69 us: per_device(): return (outputs, jnp.stack([first_log, second_log]))]
    reduce_sum x1, other arithmetic: 2.76 us -> 0.87 us  [masked_log_probs(): jnp.sum(jnp.where(allowed, jnp.exp(shifted), 0.0), -1, keepdims=True)]
where the time goes in v2:
time: 171 us; the launch traced here: 170 us
  Pallas kernels  148 us (87%)
  other arithmetic  12.1 us (7%)
  matrix products  4.08 us (2%)
  local copies, waits for them, and re-layouts  3.77 us (2%)
  between operations  2.18 us (1%)
    pallas_call x5, Pallas kernels, project(): pl.pallas_call(functools.partial(project_kernel, nx, ny, head, tile), out...  148 us

profile of v2, /device:TPU:0, one launch (start us, length us, event | category | flops | bytes accessed | tf_op | source)
XLA Modules:
  0.0 170.0 jit_solution(11467148488737118875)
XLA Ops:
  1.4 0.8 mul.182
  2.2 0.9 fusion.42
  3.1 1.5 fusion.46.x_ref
  4.6 27.3 %shard_map.158 = bf16[2,10240]{1,0:T(2,128)(2,1)} custom-call(bf16[4,2,2048]{2,1,0:T(2,128)(2,1)} %fusion.46.x_ref, bf16[2048,1280]{1,0:T(8,128)(2,1)} %w_ref.5), custom_call_target="tpu_custom_call" | custom-call | flops 335544320 | bytes 5242880 | tf_op jit(solution)/shard_map/pallas_call | solution.py:289
  31.9 0.8 convert_bitcast_fusion
  32.8 0.7 bitcast_convert_fusion
  33.9 0.6 copy.47
  34.6 0.8 fusion.63
  36.1 0.6 copy.48
  36.8 0.7 fusion.16
  37.5 1.0 fusion.20
  38.5 0.6 copy.76
  39.1 23.0 %shard_map.159 = bf16[2,8192]{1,0:T(2,128)(2,1)} custom-call(bf16[4,2,2048]{2,1,0:T(2,128)(2,1)} %bitcast.116, bf16[2048,1024]{1,0:T(8,128)(2,1)} %w_ref.6), custom_call_target="tpu_custom_call" | custom-call | flops 268435456 | bytes 4194304 | tf_op jit(solution)/shard_map/pallas_call | solution.py:289
  62.2 0.9 fusion.38
  63.1 1.5 fusion.40
  64.6 33.1 %shard_map.160 = bf16[2,57344]{1,0:T(2,128)(2,1)} custom-call(bf16[4,2,2048]{2,1,0:T(2,128)(2,1)} %bitcast.117, bf16[2048,7168]{1,0:T(8,128)(2,1)} %w_ref.7), custom_call_target="tpu_custom_call" | custom-call | flops 1879048192 | bytes 29360128 | tf_op jit(solution)/shard_map/pallas_call | solution.py:289
  97.7 1.9 %fusion.32 = bf16[2,28672]{1,0:T(2,128)(2,1)} fusion(bf16[2,57344]{1,0:T(2,128)(2,1)} %shard_map.160), kind=kLoop, calls=%fused_computation.31 | loop fusion | flops 458752 | bytes 344064 | tf_op jit(solution)/shard_map/convert_element_type | solution.py:431
  99.6 46.6 %shard_map.161 = bf16[2,8192]{1,0:T(2,128)(2,1)} custom-call(bf16[4,2,7168]{2,1,0:T(2,128)(2,1)} %bitcast.115, bf16[7168,1024]{1,0:T(8,128)(2,1)} %w_ref.8), custom_call_target="tpu_custom_call" | custom-call | flops 939524096 | bytes 14680064 | tf_op jit(solution)/shard_map/pallas_call | solution.py:289
  146.2 1.0 fusion.35
  147.2 0.7 fusion.37
  147.9 17.9 %shard_map.162 = f32[2,512]{1,0:T(2,128)} custom-call(bf16[4,2,2048]{2,1,0:T(2,128)(2,1)} %bitcast.118, bf16[256,512]{1,0:T(8,128)(2,1)} %w_ref.9), custom_call_target="tpu_custom_call" | custom-call | flops 16777216 | bytes 262144 | tf_op jit(solution)/shard_map/pallas_call | solution.py:289
  166.8 1.0 select_reduce_fusion.1
  167.8 0.9 select_reduce_fusion
  168.7 0.8 select_bitcast_fusion
  (43 shorter events, 2.4 us)
Async XLA Ops:
  4.6 29.3 %copy-start = (bf16[1,1024,1024]{2,1,0:T(8,128)(2,1)S(1)}, bf16[1,1024,1024]{2,1,0:T(8,128)(2,1)}, u32[]{:S(2)}) copy-start(bf16[1,1024,1024]{2,1,0:T(8,128)(2,1)} %param.16) | copy-start | bytes 6291460
  34.5 1.6 copy-start.1
  39.1 23.0 %copy-start.2 = (bf16[2,1,8192]{2,0,1:T(2,128)(2,1)S(1)}, bf16[2,1,8192]{2,0,1:T(2,128)(2,1)}, u32[]{:S(2)}) copy-start(bf16[2,1,8192]{2,0,1:T(2,128)(2,1)} %param.15) | copy-start | bytes 98308
  39.1 24.0 %copy-start.6 = (f32[8192]{0:T(1024)S(1)}, f32[8192]{0:T(1024)}, u32[]{:S(2)}) copy-start(f32[8192]{0:T(1024)} %param.25) | copy-start | bytes 98308
  99.5 46.6 %copy-start.3 = (bf16[2,8192]{1,0:T(2,128)(2,1)S(1)}, bf16[2,8192]{1,0:T(2,128)(2,1)}, u32[]{:S(2)}) copy-start(bf16[2,8192]{1,0:T(2,128)(2,1)} %shard_map.159) | copy-start | bytes 98308
  99.5 47.6 %copy-start.5 = (f32[8192]{0:T(1024)S(1)}, f32[8192]{0:T(1024)}, u32[]{:S(2)}) copy-start(f32[8192]{0:T(1024)} %param.28) | copy-start | bytes 98308
  99.5 66.9 %copy-start.7 = (s32[512]{0:T(512)S(1)}, s32[512]{0:T(512)}, u32[]{:S(2)}) copy-start(s32[512]{0:T(512)} %param.20) | copy-start | bytes 6148
  99.5 66.9 %copy-start.8 = (s32[1,16]{1,0:T(1,128)S(1)}, s32[1,16]{1,0:T(1,128)}, u32[]{:S(2)}) copy-start(s32[1,16]{1,0:T(1,128)} %param.19) | copy-start | bytes 196
  147.1 22.9 %copy-start.4 = (bf16[2,8192]{1,0:T(2,128)(2,1)}, bf16[2,8192]{1,0:T(2,128)(2,1)S(1)}, u32[]{:S(2)}) copy-start(bf16[2,8192]{1,0:T(2,128)(2,1)S(1)} %get-tuple-element.7) | copy-start | bytes 98308
